TPU v7x, 128 devices: a whole 4x4x4 slice. The times are simulated.
128 devices in a mesh: row: 8 (over y, z_lo), col: 16 (over z_hi, x, core).
Axes of the slice: x: 4, y: 4, z: 4 (z_hi: 2, z_lo: 2; z = z_hi * 2 + z_lo), core: 2. Of those that a mesh axis runs over, the one named last changes fastest.
Arguments:
- features: bfloat16 [32768, 512], P(('row', 'col')), may hold values from -6 to 6
- adj_values: bfloat16 [8, 16, 32, 256, 256], P('row', 'col'), may hold values from -0.0625 to 0.0625
- block_cells: int32 [8, 16, 32], P('row', 'col'), may hold values from 0 to 127, as said below
- block_counts: int32 [8, 16], P('row', 'col'), may hold values from 8 to 32, as said below
- w_first: bfloat16 [512, 512], replicated, may hold values from -0.25 to 0.25
- w_second: bfloat16 [512, 512], replicated, may hold values from -0.25 to 0.25
- cotangent: bfloat16 [32768, 512], P(('row', 'col')), may hold values from -6 to 6
Outputs:
- out_act: bfloat16 [32768, 512], P(('row', 'col'))
- grad_input: bfloat16 [32768, 512], P(('row', 'col'))
- grad_first: float32 [512, 512], replicated
- grad_second: float32 [512, 512], replicated
Inputs may be any that keep to these rules, and one draw needn't show every extreme that they name: `block_cells`: within one tile the listed positions are distinct; each lies in 0 to 8 * 16 * 1^2 - 1. `block_counts`: some tile lists 32 live blocks.
All inputs are finite; a program needn't handle non-finite values.
Results may differ from a plain program's by a relative error of at most 0.034.
Values may be sent and summed in bfloat16 or wider, within the bound.
A program may use at most 128 MiB of HBM per device.

v0:
```python
import jax
import jax.numpy as jnp
from jax import lax
from jax.sharding import PartitionSpec as P


def silu_slope(pre):
    sig = jax.nn.sigmoid(pre)
    return sig * (1.0 + pre * (1.0 - sig))


def tile_range(values, cells, live_count, source, first_block, n_blocks, block_cols, transposed):
    rows_blk = cells // block_cols
    cols_blk = cells % block_cols
    if transposed:
        take_idx, put_idx = (rows_blk, cols_blk)
    else:
        take_idx, put_idx = (cols_blk, rows_blk)

    def advance(group, total):
        begin = group * 8
        for offset in range(8):
            slot = begin + offset
            put = put_idx[slot] - first_block
            wanted = (slot < live_count) & (put >= 0) & (put < n_blocks)

            def add_block(current):
                block = lax.dynamic_index_in_dim(values, slot, 0, keepdims=False)
                picked = lax.dynamic_index_in_dim(source, take_idx[slot], 0, keepdims=False)
                if transposed:
                    product = lax.dot_general(
                        block, picked, (((0,), (0,)), ((), ())), preferred_element_type=jnp.float32
                    )
                else:
                    product = jnp.dot(block, picked, preferred_element_type=jnp.float32)
                place = jnp.clip(put, 0, n_blocks - 1)
                old = lax.dynamic_index_in_dim(current, place, 0, keepdims=False)
                return lax.dynamic_update_index_in_dim(current, old + product, place, 0)

            total = lax.cond(wanted, add_block, lambda current: current, total)
        return total

    start = jnp.zeros((n_blocks, source.shape[1], source.shape[2]), jnp.float32)
    finish = values.shape[0] // 8
    return lax.fori_loop(0, finish, advance, start)


def aggregate(local_rows, values, cells, live_count):
    n_row = lax.axis_size("row")
    n_col = lax.axis_size("col")
    nodes_dev, width = local_rows.shape
    side = values.shape[1]
    block_rows = n_col * nodes_dev // side
    block_cols = n_row * nodes_dev // side
    colsrc = lax.all_gather(local_rows, "row", axis=0, tiled=True).reshape(block_cols, side, width)
    partial_value = tile_range(values, cells, live_count, colsrc, 0, block_rows, block_cols, False)
    partial_value = partial_value.reshape(block_rows * side, width)
    return lax.psum_scatter(
        partial_value.astype(jnp.bfloat16), "col", scatter_dimension=0, tiled=True
    ).astype(jnp.float32)


def aggregate_back(local_rows, values, cells, live_count):
    n_row = lax.axis_size("row")
    n_col = lax.axis_size("col")
    nodes_dev, width = local_rows.shape
    side = values.shape[1]
    block_rows = n_col * nodes_dev // side
    block_cols = n_row * nodes_dev // side
    rowsrc = lax.all_gather(local_rows, "col", axis=0, tiled=True).reshape(block_rows, side, width)
    partial_value = tile_range(values, cells, live_count, rowsrc, 0, block_cols, block_cols, True)
    partial_value = partial_value.reshape(block_cols * side, width)
    return lax.psum_scatter(
        partial_value.astype(jnp.bfloat16), "row", scatter_dimension=0, tiled=True
    ).astype(jnp.float32)


def local(features, adj_values, block_cells, block_counts, w_first, w_second, cotangent):
    values = adj_values[0, 0]
    cells = block_cells[0, 0]
    live_count = block_counts[0, 0]
    agg_first = aggregate(features, values, cells, live_count).astype(jnp.bfloat16)
    pre_first = jnp.dot(agg_first, w_first, preferred_element_type=jnp.float32)
    hidden = jax.nn.silu(pre_first).astype(jnp.bfloat16)
    agg_second = aggregate(hidden, values, cells, live_count).astype(jnp.bfloat16)
    pre_second = jnp.dot(agg_second, w_second, preferred_element_type=jnp.float32)
    out_act = jax.nn.silu(pre_second).astype(jnp.bfloat16)
    d_second = (cotangent.astype(jnp.float32) * silu_slope(pre_second)).astype(jnp.bfloat16)
    local_second = lax.dot_general(
        agg_second, d_second, (((0,), (0,)), ((), ())), preferred_element_type=jnp.float32
    )
    grad_second = lax.psum(local_second, ("row", "col"))
    back_second = lax.dot_general(
        d_second, w_second, (((1,), (1,)), ((), ())), preferred_element_type=jnp.float32
    ).astype(jnp.bfloat16)
    d_hidden = aggregate_back(back_second, values, cells, live_count)
    d_first = (d_hidden * silu_slope(pre_first)).astype(jnp.bfloat16)
    local_first = lax.dot_general(
        agg_first, d_first, (((0,), (0,)), ((), ())), preferred_element_type=jnp.float32
    )
    grad_first = lax.psum(local_first, ("row", "col"))
    back_first = lax.dot_general(
        d_first, w_first, (((1,), (1,)), ((), ())), preferred_element_type=jnp.float32
    ).astype(jnp.bfloat16)
    grad_input = aggregate_back(back_first, values, cells, live_count).astype(jnp.bfloat16)
    return (out_act, grad_input, grad_first, grad_second)


def solution(mesh):
    return jax.shard_map(
        local,
        mesh=mesh,
        in_specs=(
            P(("row", "col"), None),
            P("row", "col", None, None, None),
            P("row", "col", None),
            P("row", "col"),
            P(),
            P(),
            P(("row", "col"), None),
        ),
        out_specs=(P(("row", "col"), None), P(("row", "col"), None), P(), P()),
        check_vma=False,
    )
```

profile of v0, /device:TPU:1, one launch (start us, length us, event | category | flops | bytes accessed | tf_op | source)
XLA Modules:
  0.0 1583.5 jit_solution(1694215078316335465)
XLA Ops:
  8.6 53.5 %all-gather.5.cloned.1.call-done = bf16[2048,512]{1,0:T(8,128)(2,1)} async-done(((bf16[256,512]{1,0:T(8,128)(2,1)}), bf16[2048,512]{1,0:T(8,128)(2,1)}) %all-gather.5.cloned.1.call-update) | async-done | bytes 2097168 | tf_op jit(solution)/shard_map/all_gather | solution.py:55
  66.6 120.6 %while.72 = (s32[]{:T(128)}, f32[16,256,512]{2,1,0:T(8,128)}, s32[]{:T(128)}, s32[32]{0:T(128)S(1)}, bf16[32,256,256]{2,1,0:T(8,128)(2,1)}, /*index=5*/s32[32]{0...) while((s32[]{:T(128)}, f32[16,256,512]{2,1,0:T(8,128)}, ...), condition=%wide.region_17.18_spmd, body=%wide.region_0.17_spmd.sunk | while | flops 537919616 | bytes 19925340 | solution.py:45
  77.5 6.4 conditional.65
  193.3 221.2 %reduce-scatter.5.cloned.1.call-done = bf16[256,512]{1,0:T(8,128)(2,1)} async-done(((bf16[4096,512]{1,0:T(8,128)(2,1)}), bf16[256,512]{1,0:T(8,128)(2,1)}) %reduce-scatter.5.cloned.1.call-update) | async-done | bytes 262160 | tf_op jit(solution)/shard_map/reduce_scatter | solution.py:58
  416.7 49.3 %all-gather.7.cloned.1.call-done = bf16[2048,512]{1,0:T(8,128)(2,1)} async-done(((bf16[256,512]{1,0:T(8,128)(2,1)}), bf16[2048,512]{1,0:T(8,128)(2,1)}) %all-gather.7.cloned.1.call-update) | async-done | bytes 2097168 | tf_op jit(solution)/shard_map/all_gather | solution.py:55
  470.4 119.7 %while.73 = (s32[]{:T(128)}, f32[16,256,512]{2,1,0:T(8,128)}, s32[]{:T(128)}, s32[32]{0:T(128)S(1)}, bf16[32,256,256]{2,1,0:T(8,128)(2,1)}, /*index=5*/s32[32]{0...) while((s32[]{:T(128)}, f32[16,256,512]{2,1,0:T(8,128)}, ...), condition=%wide.region_36.37_spmd, body=%wide.region_19.36_spmd.sunk | while | flops 537919616 | bytes 19925340 | solution.py:45
  473.1 6.4 conditional.72
  481.5 6.4 conditional.73
  513.5 6.4 conditional.77
  538.5 6.4 conditional.72
  596.2 220.4 %reduce-scatter.7.cloned.1.call-done = bf16[256,512]{1,0:T(8,128)(2,1)} async-done(((bf16[4096,512]{1,0:T(8,128)(2,1)}), bf16[256,512]{1,0:T(8,128)(2,1)}) %reduce-scatter.7.cloned.1.call-update) | async-done | bytes 262160 | tf_op jit(solution)/shard_map/reduce_scatter | solution.py:58
  819.9 56.4 %all-gather.9.cloned.1.call-done = bf16[4096,512]{1,0:T(8,128)(2,1)} async-done(((bf16[256,512]{1,0:T(8,128)(2,1)}), bf16[4096,512]{1,0:T(8,128)(2,1)}) %all-gather.9.cloned.1.call-update) | async-done | bytes 4194320 | tf_op jit(solution)/shard_map/all_gather | solution.py:70
  878.9 120.2 %while.74 = (s32[]{:T(128)}, f32[8,256,512]{2,1,0:T(8,128)}, s32[]{:T(128)}, s32[32]{0:T(128)S(1)}, bf16[32,256,256]{2,1,0:T(8,128)(2,1)}, /*index=5*/s32[32]{0:...) while((s32[]{:T(128)}, f32[8,256,512]{2,1,0:T(8,128)}, ...), condition=%wide.region_55.56_spmd, body=%wide.region_38.55_spmd.sunk | while | flops 537919616 | bytes 19925332 | solution.py:45
  889.9 6.5 conditional.81
  922.2 6.5 conditional.85
  947.5 6.4 conditional.80
  1003.1 189.1 %reduce-scatter.9.cloned.1.call-done = bf16[256,512]{1,0:T(8,128)(2,1)} async-done(((bf16[2048,512]{1,0:T(8,128)(2,1)}), bf16[256,512]{1,0:T(8,128)(2,1)}) %reduce-scatter.9.cloned.1.call-update) | async-done | bytes 262160 | tf_op jit(solution)/shard_map/reduce_scatter | solution.py:73
  1197.3 56.0 %all-gather.11.cloned.1.call-done = bf16[4096,512]{1,0:T(8,128)(2,1)} async-done(((bf16[256,512]{1,0:T(8,128)(2,1)}), bf16[4096,512]{1,0:T(8,128)(2,1)}) %all-gather.11.cloned.1.call-update) | async-done | bytes 4194320 | tf_op jit(solution)/shard_map/all_gather | solution.py:70
  1255.8 121.9 %while.75 = (s32[]{:T(128)}, f32[8,256,512]{2,1,0:T(8,128)}, s32[]{:T(128)}, s32[32]{0:T(128)S(1)}, bf16[32,256,256]{2,1,0:T(8,128)(2,1)}, /*index=5*/s32[32]{0:...) while((s32[]{:T(128)}, f32[8,256,512]{2,1,0:T(8,128)}, ...), condition=%wide.region_74.75_spmd, body=%wide.region_57.74_spmd.sunk | while | flops 537919616 | bytes 19925332 | solution.py:45
  1274.7 6.4 conditional.90
  1291.2 6.6 conditional.92
  1316.1 6.5 conditional.95
  1381.6 26.1 %all-reduce.3.cloned.1.call-done = (f32[512,512]{1,0:T(8,128)}, f32[512,512]{1,0:T(8,128)}) async-done(((f32[512,512]{1,0:T(8,128)}, f32[512,512]{1,0:T(8,128)}), (f32[512,512]{1,0:T(8,128)}, f32[512,512]{1,0:T(8,128)})) %all-reduce.3.cloned.1.call-update) | async-done | bytes 2097168 | tf_op jit(solution)/shard_map/psum | solution.py:101
  1407.7 164.7 %reduce-scatter.11.cloned.1.call-done = bf16[256,512]{1,0:T(8,128)(2,1)} async-done(((bf16[2048,512]{1,0:T(8,128)(2,1)}), bf16[256,512]{1,0:T(8,128)(2,1)}) %reduce-scatter.11.cloned.1.call-update) | async-done | bytes 262160 | tf_op jit(solution)/shard_map/reduce_scatter | solution.py:73
  (295 shorter events, 351.2 us)
Async XLA Ops:
  7.2 809.5 %copy-start = (bf16[512,512]{1,0:T(8,128)(2,1)S(1)}, bf16[512,512]{1,0:T(8,128)(2,1)}, u32[]{:S(2)}) copy-start(bf16[512,512]{1,0:T(8,128)(2,1)} %param.84) | copy-start | bytes 1572868
  7.2 55.0 %all-gather.5.cloned.1.call-start = ((), (), s32[]{:S(2)}) async-start(), calls=%async_computation.4 | async-start | bytes 2359296 | tf_op jit(solution)/shard_map/all_gather | solution.py:55
  7.9 406.5 %reduce-scatter.5.cloned.1.call-start = ((), (), s32[]{:S(2)}) async-start(), calls=%async_computation.5 | async-start | bytes 4456448 | tf_op jit(solution)/shard_map/reduce_scatter | solution.py:58
  62.1 4.4 copy-start.2
  193.2 221.2 %copy-start.4 = (bf16[512,512]{1,0:T(8,128)(2,1)S(1)}, bf16[512,512]{1,0:T(8,128)(2,1)}, u32[]{:S(2)}) copy-start(bf16[512,512]{1,0:T(8,128)(2,1)} %param.83) | copy-start | bytes 1572868
  193.2 272.8 %all-gather.7.cloned.1.call-start = ((), (), s32[]{:S(2)}) async-start(), calls=%async_computation.6 | async-start | bytes 2359296 | tf_op jit(solution)/shard_map/all_gather | solution.py:55
  416.6 400.0 %reduce-scatter.7.cloned.1.call-start = ((), (), s32[]{:S(2)}) async-start(), calls=%async_computation.7 | async-start | bytes 4456448 | tf_op jit(solution)/shard_map/reduce_scatter | solution.py:58
  466.0 4.4 copy-start.3
  596.2 220.5 %copy-start.8 = (bf16[256,512]{1,0:T(8,128)(2,1)S(1)}, bf16[256,512]{1,0:T(8,128)(2,1)}, u32[]{:S(2)}) copy-start(bf16[256,512]{1,0:T(8,128)(2,1)} %param.85) | copy-start | bytes 786436
  596.2 280.1 %all-gather.9.cloned.1.call-start = ((), (), s32[]{:S(2)}) async-start(), calls=%async_computation.8 | async-start | bytes 4456448 | tf_op jit(solution)/shard_map/all_gather | solution.py:70
  819.8 372.3 %reduce-scatter.9.cloned.1.call-start = ((), (), s32[]{:S(2)}) async-start(), calls=%async_computation.9 | async-start | bytes 2359296 | tf_op jit(solution)/shard_map/reduce_scatter | solution.py:73
  999.1 193.0 %copy-start.5 = (f32[256,512]{1,0:T(8,128)S(1)}, f32[256,512]{1,0:T(8,128)}, u32[]{:S(2)}) copy-start(f32[256,512]{1,0:T(8,128)} %get-tuple-element.1759) | copy-start | bytes 1572868
  999.1 195.3 %copy-start.7 = (bf16[256,512]{1,0:T(8,128)(2,1)S(1)}, bf16[256,512]{1,0:T(8,128)(2,1)}, u32[]{:S(2)}) copy-start(bf16[256,512]{1,0:T(8,128)(2,1)} %reduce-scatter.7.cloned.1.call-done) | copy-start | bytes 786436
  1003.0 192.7 %copy-start.6 = (bf16[256,512]{1,0:T(8,128)(2,1)S(1)}, bf16[256,512]{1,0:T(8,128)(2,1)}, u32[]{:S(2)}) copy-start(bf16[256,512]{1,0:T(8,128)(2,1)} %reduce-scatter.5.cloned.1.call-done) | copy-start | bytes 786436
  1003.0 250.2 %all-gather.11.cloned.1.call-start = ((), (), s32[]{:S(2)}) async-start(), calls=%async_computation.10 | async-start | bytes 4456448 | tf_op jit(solution)/shard_map/all_gather | solution.py:70
  1194.4 213.4 %all-reduce.3.cloned.1.call-start = ((), (), s32[]{:S(2)}) async-start(), calls=%async_computation.12 | async-start | bytes 4194304 | tf_op jit(solution)/shard_map/psum | solution.py:101
  1197.1 375.4 %reduce-scatter.11.cloned.1.call-start = ((), (), s32[]{:S(2)}) async-start(), calls=%async_computation.11 | async-start | bytes 2359296 | tf_op jit(solution)/shard_map/reduce_scatter | solution.py:73
  1377.7 199.3 %copy-start.1 = (bf16[512,512]{1,0:T(8,128)(2,1)S(1)}, bf16[512,512]{1,0:T(8,128)(2,1)}, u32[]{:S(2)}) copy-start(bf16[512,512]{1,0:T(8,128)(2,1)} %param.84) | copy-start | bytes 1572868
Sparse Core Ops, SparseCore 0:
  9.7 52.4 all-gather.4
  193.3 221.0 reduce-scatter.4
  416.8 49.1 all-gather.6
  596.3 220.2 reduce-scatter.6
  819.9 56.3 all-gather.8
  1003.2 188.9 reduce-scatter.8
  1195.2 58.0 all-gather.10
  1258.8 148.8 all-reduce.2
  1410.7 161.7 reduce-scatter.10
where the time goes:
time: 1600 us; the launch traced here: 1580 us
  waiting for transfers between devices  1040 us (65%)
  loops' own time  338 us (21%)
  local copies, waits for them, and re-layouts  90.6 us (6%)
  matrix products  81.7 us (5%)
  other arithmetic  21.7 us (1%)
    reduce_scatter x2, waiting for transfers between devices, aggregate(): lax.psum_scatter(partial_value.astype(jnp.bfloat16), 'col', scatter_dimen...  442 us
    reduce_scatter x2, waiting for transfers between devices, aggregate_back(): lax.psum_scatter(partial_value.astype(jnp.bfloat16), 'row', scatter_dimen...  354 us
    another operation x4, loops' own time, tile_range(): return lax.fori_loop(0, finish, advance, start)  245 us
    all_gather x2, waiting for transfers between devices, aggregate_back(): lax.all_gather(local_rows, 'col', axis=0, tiled=True)  112 us
    all_gather x2, waiting for transfers between devices, aggregate(): lax.all_gather(local_rows, 'row', axis=0, tiled=True)  103 us
    another operation x128, loops' own time, advance(): total = lax.cond(wanted, add_block, lambda current: current, total)  92.9 us
    dynamic_slice x36, local copies, waits for them, and re-layouts, add_block(): old = lax.dynamic_index_in_dim(current, place, 0, keepdims=False)  38.9 us
    dot_general x18, matrix products, add_block(): lax.dot_general(block, picked, (((0,), (0,)), ((), ())), preferred_elemen...  37.7 us
  transfers between devices with their start and end apart: 9, of which 9 were waited for; matrix products, arithmetic and copies ran while one was open for 3% of the time, Pallas kernels for 0%

commit v1 on v0

v1 whole, which is shorter than its diff:
```python
import functools

import jax
import jax.numpy as jnp
from jax import lax
from jax.experimental import pallas as pl
from jax.experimental.pallas import tpu as pltpu
from jax.sharding import PartitionSpec as P

MESH = pl.DeviceIdType.MESH
BF = jnp.bfloat16
F32 = jnp.float32
N_SEM = 360


def slot_plan(cells, live_count, block_cols, n_out, transposed):
    n = cells.shape[0]
    ids = jnp.arange(n, dtype=jnp.int32)
    rows, cols = cells // block_cols, cells % block_cols
    take, put = (rows, cols) if transposed else (cols, rows)
    put = jnp.where(ids < live_count, put, n_out)
    key = put * n + ids
    rank = jnp.sum((key[None, :] < key[:, None]).astype(jnp.int32), axis=1)
    hot = (rank[None, :] == ids[:, None]).astype(jnp.int32)
    order = jnp.sum(hot * ids[None, :], axis=1)
    takes = jnp.sum(hot * take[None, :], axis=1)
    first = jnp.sum((put[None, :] == put[:, None]) & (ids[None, :] < ids[:, None]), axis=1) == 0
    keep = jnp.sum(hot * jnp.where(first, 0, 1)[None, :], axis=1)
    outs = jnp.arange(16, dtype=jnp.int32)
    here = jnp.sum((put[None, :] == outs[:, None]).astype(jnp.int32), axis=1)
    upto = jnp.sum((put[None, :] <= outs[:, None]).astype(jnp.int32), axis=1)
    last = jnp.where(here > 0, upto - 1, n)
    return jnp.concatenate([order, takes, keep, last])


class Ring:
    def __init__(self, ring, pair, slot, device):
        self.ring, self.pair = ring, pair
        self.slot_of, self.device_of = slot, device

    def at(self, dr, dp):
        return lax.rem(self.ring + dr, 4), (1 - self.pair) if dp else self.pair

    def slot(self, dr, dp, **kw):
        return self.slot_of(*self.at(dr, dp), **kw)

    def device(self, dr, dp):
        return self.device_of(*self.at(dr, dp))


class Net:
    def __init__(self, send_sems, recv_sems):
        self.send_sems, self.recv_sems = send_sems, recv_sems
        self.used = 0
        self.open = {}

    def send(self, src, dst, device, group):
        i = self.used
        self.used += 1
        copy = pltpu.make_async_remote_copy(
            src_ref=src,
            dst_ref=dst,
            send_sem=self.send_sems.at[i],
            recv_sem=self.recv_sems.at[i],
            device_id=device,
            device_id_type=MESH,
        )
        copy.start()
        self.open.setdefault(group, []).append(copy)
        return copy

    def drain(self, group):
        for copy in self.open.pop(group, []):
            copy.wait_send()


def gather(net, geo, x, partner=None):
    half = x.shape[1] // 2
    low, high = pl.ds(0, half), pl.ds(half, half)
    right, left, pair = geo.device(1, 0), geo.device(3, 0), geo.device(0, 1)
    shares = []

    def share(dr, dp):
        if partner is not None:
            ref = x.at[geo.slot(dr, dp)]
            shares.append(net.send(ref, ref, partner, "x"))

    def spread(dp):
        ref = x.at[geo.slot(0, dp)]
        return net.send(ref, ref, right, "x"), net.send(ref, ref, left, "x")

    def forward(dp, from_left, from_right):
        from_left.wait_recv()
        ref = x.at[geo.slot(3, dp), low]
        a = net.send(ref, ref, right, "x")
        share(3, dp)
        from_right.wait_recv()
        ref = x.at[geo.slot(1, dp), high]
        b = net.send(ref, ref, left, "x")
        share(1, dp)
        return a, b

    ref = x.at[geo.slot(0, 0)]
    across = net.send(ref, ref, pair, "x")
    own = spread(0)
    share(0, 0)
    yield
    far_own = forward(0, *own)
    yield
    across.wait_recv()
    other = spread(1)
    share(0, 1)
    yield
    far_other = forward(1, *other)
    yield
    for c in far_own:
        c.wait_recv()
    share(2, 0)
    for c in far_other:
        c.wait_recv()
    share(2, 1)
    for c in shares:
        c.wait_recv()
    yield


ORDER = ((2, 1), (1, 1), (3, 1), (2, 0), (1, 0), (3, 0), (0, 1), (0, 0))
GROUPS = ((0, 3), (3, 3), (6, 2))


def place(dr, dp):
    return ORDER.index((dr, dp))


def scatter(net, geo, pick, s, buf, group, done, partner=None, t=None, rc=None):
    ra, rb, rd, total = buf
    half = s.shape[1] // 2
    low, high = pl.ds(0, half), pl.ds(half, half)
    right, left, pair = geo.device(1, 0), geo.device(3, 0), geo.device(0, 1)
    net.drain(group)
    cores = []
    if partner is not None:
        for begin, count in GROUPS:
            for i in range(begin, begin + count):
                t[i] = pick(geo.slot(*ORDER[i], other=True))
            cores.append(net.send(t.at[pl.ds(begin, count)], rc.at[pl.ds(begin, count)], partner, group))
    for i in range(8):
        s[i] = pick(geo.slot(*ORDER[i]))
    if partner is not None:
        yield
    first, near = {}, {}
    for dp in (1, 0):
        if partner is not None:
            g = 0 if dp else 1
            cores[g].wait_recv()
            for i in range(GROUPS[g][0], sum(GROUPS[g])):
                s[i] = (s[i].astype(F32) + rc[i].astype(F32)).astype(BF)
        far, to_r, to_l = s.at[place(2, dp)], s.at[place(1, dp)], s.at[place(3, dp)]
        first[dp] = (
            net.send(far.at[low], ra.at[dp, 0], right, group),
            net.send(far.at[high], ra.at[dp, 1], left, group),
        )
        near[dp] = [
            net.send(to_r.at[high], rb.at[dp, 0, 1], right, group),
            net.send(to_l.at[low], rb.at[dp, 1, 0], left, group),
        ]
    if partner is not None:
        cores[2].wait_recv()
        for i in (6, 7):
            s[i] = (s[i].astype(F32) + rc[i].astype(F32)).astype(BF)
    yield
    for dp in (1, 0):
        to_r, to_l = place(1, dp), place(3, dp)
        first[dp][0].wait_recv()
        s[to_r, low] = (s[to_r, low].astype(F32) + ra[dp, 0].astype(F32)).astype(BF)
        near[dp].append(net.send(s.at[to_r, low], rb.at[dp, 0, 0], right, group))
        first[dp][1].wait_recv()
        s[to_l, high] = (s[to_l, high].astype(F32) + ra[dp, 1].astype(F32)).astype(BF)
        near[dp].append(net.send(s.at[to_l, high], rb.at[dp, 1, 1], left, group))
    yield

    def come(dp, h):
        rows = (low, high)[h]
        return s[place(0, dp), rows].astype(F32) + rb[dp, 0, h].astype(F32) + rb[dp, 1, h].astype(F32)

    for c in near[1]:
        c.wait_recv()
    for h in range(2):
        s[place(0, 1), (low, high)[h]] = come(1, h).astype(BF)
    last = net.send(s.at[place(0, 1)], rd, pair, group)
    yield
    for c in near[0]:
        c.wait_recv()
    for h in range(2):
        total[(low, high)[h]] = come(0, h)
    yield
    last.wait_recv()
    done(total[...] + rd[...].astype(F32))
    yield


def all_reduce(net, g, bufs, where, out):
    x, y, z, core, dev_x, dev_y, dev_z, partner = where
    b1, r1, h1, b2, r2, h2, b3, r3, h3, b4, r4, gb = bufs
    n = h1.shape[0]
    mine = pl.ds(pl.multiple_of(core * n, n), n)
    his = pl.ds(pl.multiple_of((1 - core) * n, n), n)
    b1[...] = g[his, :].astype(BF)
    c = net.send(b1, r1, partner, "g")
    yield
    c.wait_recv()
    h1[...] = g[mine, :] + r1[...].astype(F32)
    m = h2.shape[0]
    for k in range(4):
        b2[k] = h1[pl.ds(k * m, m), :].astype(BF)
    cs = [net.send(b2.at[lax.rem(x + d, 4)], r2.at[d - 1], dev_x(d), "g") for d in (1, 2, 3)]
    yield
    for c in cs:
        c.wait_recv()
    h2[...] = h1[pl.ds(pl.multiple_of(x * m, m), m), :] + r2[0].astype(F32) + r2[1].astype(F32) + r2[2].astype(F32)
    m = h3.shape[0]
    for k in range(4):
        b3[k] = h2[pl.ds(k * m, m), :].astype(BF)
    cs = [net.send(b3.at[lax.rem(y + d, 4)], r3.at[d - 1], dev_y(d), "g") for d in (1, 2, 3)]
    yield
    for c in cs:
        c.wait_recv()
    h3[...] = h2[pl.ds(pl.multiple_of(y * m, m), m), :] + r3[0].astype(F32) + r3[1].astype(F32) + r3[2].astype(F32)
    w = b4.shape[2]
    for k in range(4):
        b4[k] = h3[:, k * w : (k + 1) * w].astype(BF)
    cs = [net.send(b4.at[lax.rem(z + d, 4)], r4.at[d - 1], dev_z(d), "g") for d in (1, 2, 3)]
    yield
    for c in cs:
        c.wait_recv()
    piece = h3[:, pl.ds(pl.multiple_of(z * w, w), w)]
    piece = piece + r4[0].astype(F32) + r4[1].astype(F32) + r4[2].astype(F32)
    gb[core, x, y, z] = piece.astype(BF)
    ref = gb.at[core, x, y, z]
    cs = [net.send(ref, ref, dev_z(d), "g") for d in (1, 2, 3)]
    yield
    for c in cs:
        c.wait_recv()
    ref = gb.at[core, x, y]
    cs = [net.send(ref, ref, dev_y(d), "g") for d in (1, 2, 3)]
    yield
    for c in cs:
        c.wait_recv()
    ref = gb.at[core, x]
    cs = [net.send(ref, ref, dev_x(d), "g") for d in (1, 2, 3)]
    yield
    for c in cs:
        c.wait_recv()
    ref = gb.at[core]
    c = net.send(ref, ref, partner, "g")
    yield
    c.wait_recv()
    m = h3.shape[0]

    def write(i, carry):
        for k in range(4):
            begin = pl.multiple_of(i * m, m)
            out[pl.ds(begin, m), k * w : (k + 1) * w] = gb[i // 16, lax.rem(i // 4, 4), lax.rem(i, 4), k].astype(F32)
        return carry

    lax.fori_loop(0, 32, write, 0)
    yield


def slope(pre):
    sig = jax.nn.sigmoid(pre)
    return sig * (1.0 + pre * (1.0 - sig))


def dot_rows(a, b):
    return lax.dot_general(a, b, (((0,), (0,)), ((), ())), preferred_element_type=F32)


def dot_cols(a, b):
    return lax.dot_general(a, b, (((1,), (1,)), ((), ())), preferred_element_type=F32)


def dot(a, b):
    return jnp.dot(a, b, preferred_element_type=F32)


def kernel(names, plan, features, values_hbm, w_first, w_second, cotangent,
           out_act, grad_input, grad_first, grad_second, *scratch):
    m = dict(zip(names, scratch))
    row, col = lax.axis_index("row"), lax.axis_index("col")
    y, zl = row // 2, lax.rem(row, 2)
    zh, x, core = col // 8, lax.rem(col // 2, 4), lax.rem(col, 2)
    z = zh * 2 + zl

    def col_slot(r, p, other=False):
        return p * 8 + r * 2 + ((1 - core) if other else core)

    rows = Ring(y, zl, lambda r, p: r * 2 + p, lambda r, p: (r * 2 + p, col))
    cols = Ring(x, zh, col_slot, lambda r, p: (row, col_slot(r, p)))
    partner = (row, col_slot(x, zh, other=True))

    def dev_x(d):
        return cols.device(d, 0)

    def dev_y(d):
        return rows.device(d, 0)

    def dev_z(d):
        there = lax.rem(z + d, 4)
        return (y * 2 + lax.rem(there, 2), col_slot(x, there // 2))

    load = pltpu.make_async_copy(values_hbm, m["a"], m["load_sem"].at[0])
    load.start()

    barrier = pltpu.get_barrier_semaphore()
    peers = [f(d) for f in (dev_x, dev_y, dev_z) for d in (1, 2, 3)] + [partner]
    for peer in peers:
        pl.semaphore_signal(barrier, inc=1, device_id=peer, device_id_type=MESH)
    pl.semaphore_wait(barrier, len(peers))

    net = Net(m["send_sems"], m["recv_sems"])
    nl, width = features.shape
    wc = width // 2
    chunk = [slice(0, wc), slice(wc, width)]
    n_slots = m["a"].shape[0]
    prod, acc = m["prod"], m["acc"]

    def tile(a, xc, base):
        acc[...] = jnp.zeros_like(acc)

        def step(i, carry):
            p = dot(a[plan[base + i]], xc[plan[base + n_slots + i]])
            v = jnp.where(plan[base + 2 * n_slots + i] > 0, acc[...], 0.0) + p
            acc[...] = v
            prod[i] = v.astype(BF)
            return carry

        lax.fori_loop(0, n_slots, step, 0, unroll=2)

    prod[n_slots] = jnp.zeros(prod.shape[1:], BF)
    reduces = [None, None]

    def side(k, steps=1):
        if reduces[k] is not None:
            for _ in range(steps):
                next(reduces[k], None)

    def aggregate(name, back, ag, start_second, filler, done):
        a = m["at"] if back else m["a"]
        base = 3 * n_slots + 16 if back else 0
        geo = rows if back else cols

        def pick(slot):
            return prod[plan[base + 3 * n_slots + slot]]

        extra = (lambda c: {}) if back else (
            lambda c: {"partner": partner, "t": m["t", c], "rc": m["rc", name, c]}
        )
        rs = [
            scatter(
                net, geo, pick, m["s", c],
                (m["ra", name, c], m["rb", name, c], m["rd", name, c], m["total", c]),
                ("s", c), functools.partial(done, c), **extra(c),
            )
            for c in range(2)
        ]
        next(ag[0])
        start_second()
        next(ag[0])
        next(ag[0])
        next(ag[1])
        next(ag[0])
        filler()
        next(ag[0])
        tile(a, m["x", name, 0], base)
        next(rs[0])
        side(0)
        next(ag[1])
        next(ag[1])
        if not back:
            next(rs[0])
        next(ag[1])
        side(0)
        next(rs[0])
        next(ag[1])
        side(0)
        tile(a, m["x", name, 1], base)
        next(rs[1])
        next(rs[0])
        if not back:
            next(rs[1])
        side(0)
        next(rs[0])
        next(rs[1])
        side(0)
        next(rs[0])
        next(rs[1])
        side(0)
        next(rs[1])
        next(rs[1])

    def gathers(name, back):
        geo, other = (cols, partner) if back else (rows, None)
        return [gather(net, geo, m["x", name, c], other) for c in range(2)]

    agg, pre_first, pre_second, d_second, d_first = (m[k] for k in ("agg", "pre1", "pre2", "d2", "d1"))

    def own_f(name, c, value):
        m["x", name, c][rows.slot(0, 0)] = value.astype(BF)

    def own_b(name, c, value):
        m["x", name, c][cols.slot(0, 0)] = value.astype(BF)

    def layer(k, pre, w):
        def done(c, value):
            agg[k, c] = value.astype(BF)
            if c == 0:
                pre[...] = dot(agg[k, 0], w[0:wc, :])
            else:
                for n in range(2):
                    pre[:, chunk[n]] += dot(agg[k, 1], w[wc:width, chunk[n]])
                    after[k](n)
        return done

    def hidden(n):
        if n == 0:
            own_f("f2", 0, jax.nn.silu(pre_first[:, chunk[0]]))

    def output(n):
        u = pre_second[:, chunk[n]]
        out_act[:, chunk[n]] = jax.nn.silu(u).astype(BF)
        d_second[:, chunk[n]] = (cotangent[:, chunk[n]].astype(F32) * slope(u)).astype(BF)

    after = [hidden, output]

    own_f("f1", 0, features[:, chunk[0]])
    aggregate(
        "f1", False, gathers("f1", False),
        lambda: own_f("f1", 1, features[:, chunk[1]]), load.wait, layer(0, pre_first, w_first),
    )

    def turn():
        def one(i, carry):
            m["at"][i] = m["a"][i].T
            return carry
        lax.fori_loop(0, n_slots, one, 0)

    aggregate(
        "f2", False, gathers("f2", False),
        lambda: own_f("f2", 1, jax.nn.silu(pre_first[:, chunk[1]])), turn, layer(1, pre_second, w_second),
    )

    where = (x, y, z, core, dev_x, dev_y, dev_z, partner)

    def weight_grad(k, d, out, name):
        for c in range(2):
            out[chunk[c], :] = dot_rows(agg[k, c], d[...])
        bufs = [m[key, name] for key in AR_KEYS]
        g = all_reduce(net, out, bufs, where, out)
        next(g)
        return g

    def start_grad(slot, k, d, out, name):
        def run():
            reduces[slot] = weight_grad(k, d, out, name)
        return run

    def hidden_back(c, value):
        d_first[:, chunk[c]] = (value * slope(pre_first[:, chunk[c]])).astype(BF)

    own_b("b2", 0, dot_cols(d_second[...], w_second[chunk[0], :]))
    aggregate(
        "b2", True, gathers("b2", True),
        lambda: own_b("b2", 1, dot_cols(d_second[...], w_second[chunk[1], :])),
        start_grad(0, 1, d_second, grad_second, "g2"), hidden_back,
    )
    side(0, 20)

    def input_back(c, value):
        grad_input[:, chunk[c]] = value.astype(BF)

    own_b("b1", 0, dot_cols(d_first[...], w_first[chunk[0], :]))
    aggregate(
        "b1", True, gathers("b1", True),
        lambda: own_b("b1", 1, dot_cols(d_first[...], w_first[chunk[1], :])),
        start_grad(0, 0, d_first, grad_first, "g1"), input_back,
    )
    side(0, 20)
    for group in list(net.open):
        net.drain(group)


AR_KEYS = ("b1", "r1", "h1", "b2", "r2", "h2", "b3", "r3", "h3", "b4", "r4", "gb")


def scratch_of(nl, width, side, slots):
    w = width // 2
    s = {}

    def add(key, shape, kind=BF):
        s[key] = pltpu.VMEM(shape, kind)

    add("a", (slots, side, side))
    add("at", (slots, side, side))
    add("prod", (slots + 1, side, w))
    add("acc", (side, w), F32)
    for c in range(2):
        add(("s", c), (8, nl, w))
        add(("t", c), (8, nl, w))
        add(("total", c), (nl, w), F32)
        for name, blocks in (("f1", 8), ("f2", 8), ("b2", 16), ("b1", 16)):
            add(("x", name, c), (blocks, nl, w))
            add(("ra", name, c), (2, 2, nl // 2, w))
            add(("rb", name, c), (2, 2, 2, nl // 2, w))
            add(("rd", name, c), (nl, w))
            if blocks == 8:
                add(("rc", name, c), (8, nl, w))
    add("agg", (2, 2, nl, w))
    add("pre1", (nl, width), F32)
    add("pre2", (nl, width), F32)
    add("d2", (nl, width))
    add("d1", (nl, width))
    h = width
    for name in ("g2", "g1"):
        add(("b1", name), (h // 2, width))
        add(("r1", name), (h // 2, width))
        add(("h1", name), (h // 2, width), F32)
        add(("b2", name), (4, h // 8, width))
        add(("r2", name), (3, h // 8, width))
        add(("h2", name), (h // 8, width), F32)
        add(("b3", name), (4, h // 32, width))
        add(("r3", name), (3, h // 32, width))
        add(("h3", name), (h // 32, width), F32)
        add(("b4", name), (4, h // 32, width // 4))
        add(("r4", name), (3, h // 32, width // 4))
        add(("gb", name), (2, 4, 4, 4, h // 32, width // 4))
    s["load_sem"] = pltpu.SemaphoreType.DMA((1,))
    s["send_sems"] = pltpu.SemaphoreType.DMA((N_SEM,))
    s["recv_sems"] = pltpu.SemaphoreType.DMA((N_SEM,))
    return s


def local(features, adj_values, block_cells, block_counts, w_first, w_second, cotangent):
    values, cells, live = adj_values[0, 0], block_cells[0, 0], block_counts[0, 0]
    nl, width = features.shape
    slots, side, _ = values.shape
    plan = jnp.concatenate([slot_plan(cells, live, 8, 16, False), slot_plan(cells, live, 8, 8, True)])
    scratch = scratch_of(nl, width, side, slots)
    vmem = pl.BlockSpec(memory_space=pltpu.VMEM)
    return pl.pallas_call(
        functools.partial(kernel, tuple(scratch)),
        out_shape=(
            jax.ShapeDtypeStruct((nl, width), BF),
            jax.ShapeDtypeStruct((nl, width), BF),
            jax.ShapeDtypeStruct((width, width), F32),
            jax.ShapeDtypeStruct((width, width), F32),
        ),
        in_specs=[pl.BlockSpec(memory_space=pltpu.SMEM), vmem, pl.BlockSpec(memory_space=pl.ANY), vmem, vmem, vmem],
        out_specs=(vmem, vmem, vmem, vmem),
        scratch_shapes=list(scratch.values()),
        compiler_params=pltpu.CompilerParams(
            collective_id=0, has_side_effects=True, vmem_limit_bytes=63 * 1024 * 1024 - 512 * 1024
        ),
    )(plan, features, values, w_first, w_second, cotangent)


def solution(mesh):
    return jax.shard_map(
        local,
        mesh=mesh,
        in_specs=(
            P(("row", "col"), None),
            P("row", "col", None, None, None),
            P("row", "col", None),
            P("row", "col"),
            P(),
            P(),
            P(("row", "col"), None),
        ),
        out_specs=(P(("row", "col"), None), P(("row", "col"), None), P(), P()),
        check_vma=False,
    )
```

time: 1600 us -> 244 us (0.15)
  waiting for transfers between devices: 1040 us -> 0 us
  loops' own time: 338 us -> 0 us
  Pallas kernels: 0 us -> 232 us
  local copies, waits for them, and re-layouts: 90.6 us -> 8.51 us
  matrix products: 81.7 us -> 0 us
  other arithmetic: 21.7 us -> 1.74 us
    reduce_scatter x4 -> x0, waiting for transfers between devices: 795 us -> none  [the longest x2 442 us: aggregate(): lax.psum_scatter(partial_value.astype(jnp.bfloat16), 'col', scatter_dimen...]
    another operation x132 -> x0, loops' own time: 338 us -> none  [the longest x4 245 us: tile_range(): return lax.fori_loop(0, finish, advance, start)]
    pallas_call x0 -> x1, Pallas kernels: none -> 232 us  [local(): pl.pallas_call(functools.partial(kernel, tuple(scratch)), out_shape=(jax....]
    all_gather x4 -> x0, waiting for transfers between devices: 215 us -> none  [the longest x2 112 us: aggregate_back(): lax.all_gather(local_rows, 'col', axis=0, tiled=True)]
    dot_general x42 -> x0, matrix products: 81.7 us -> none  [the longest x18 37.7 us: add_block(): lax.dot_general(block, picked, (((0,), (0,)), ((), ())), preferred_elemen...]
    dynamic_slice x88 -> x0, local copies, waits for them, and re-layouts: 72.1 us -> none  [the longest x36 38.9 us: add_block(): old = lax.dynamic_index_in_dim(current, place, 0, keepdims=False)]
    psum x1 -> x0, waiting for transfers between devices: 26.1 us -> none  [local(): grad_first = lax.psum(local_first, ('row', 'col'))]
    convert_element_type x5 -> x0, other arithmetic: 21 us -> none  [the longest x2 12.1 us: aggregate(): partial_value.astype(jnp.bfloat16)]
  transfers between devices with their start and end apart: 9 -> 0, of which waited for: 9 -> 0; matrix products, arithmetic and copies ran while one was open for 3% -> 0% of each run, Pallas kernels for 0% -> 0%
where the time goes in v1:
time: 244 us; the launch traced here: 243 us
  Pallas kernels  232 us (95%)
  local copies, waits for them, and re-layouts  8.51 us (3%)
    pallas_call x1, Pallas kernels, local(): pl.pallas_call(functools.partial(kernel, tuple(scratch)), out_shape=(jax....  232 us
    unnamed x4, local copies, waits for them, and re-layouts  7.86 us

profile of v1, /device:TPU:1, one launch (start us, length us, event | category | flops | bytes accessed | tf_op | source)
XLA Modules:
  0.0 243.4 jit_solution(11342209315876801533)
XLA Ops:
  1.3 0.7 iota_add_fusion
  1.9 0.2 convert_reduce_fusion.1
  2.1 0.2 convert_reduce_fusion.3
  2.3 0.2 convert_reduce_fusion
  2.5 0.2 convert_reduce_fusion.2
  2.7 0.2 select_reduce_fusion
  2.9 0.2 convert_reduce_fusion.4
  3.1 0.7 concatenate.3.plan
  3.7 231.8 %shard_map.102 = (bf16[256,512]{1,0:T(8,128)(2,1)}, bf16[256,512]{1,0:T(8,128)(2,1)}, f32[512,512]{1,0:T(8,128)}, f32[512,512]{1,0:T(8,128)}) custom-call(s32[224]{0:T(256)} %concatenate.3.plan, bf16[256,512]{1,0:T(8,128)(2,1)} %features.1, bf16[32,256,256]{2,1,0:T(8,128)(2,1)} %bitcast.20, bf16[512,512]{1,0:T(8,128)(2,1)} %w_first.1, ...), custom_call_target="tpu_custom_call" | custom-call | tf_op jit(solution)/shard_map/pallas_call | solution.py:550
  235.5 1.7 copy.16
  237.2 1.7 copy.17
  238.8 2.3 copy.18
  241.1 2.3 copy.19
  (4 shorter events, 0.0 us)

commit v2 on v0

v2 whole, which is shorter than its diff:
```python
import functools

import jax
import jax.numpy as jnp
from jax import lax
from jax.experimental import pallas as pl
from jax.experimental.pallas import tpu as pltpu
from jax.sharding import PartitionSpec as P

MESH = pl.DeviceIdType.MESH
BF = jnp.bfloat16
F32 = jnp.float32


def slot_plan(cells, live_count, block_cols, n_out, transposed):
    n = cells.shape[0]
    ids = jnp.arange(n, dtype=jnp.int32)
    rows, cols = cells // block_cols, cells % block_cols
    take, put = (rows, cols) if transposed else (cols, rows)
    put = jnp.where(ids < live_count, put, n_out)
    key = put * n + ids
    rank = jnp.sum((key[None, :] < key[:, None]).astype(jnp.int32), axis=1)
    hot = (rank[None, :] == ids[:, None]).astype(jnp.int32)
    order = jnp.sum(hot * ids[None, :], axis=1)
    takes = jnp.sum(hot * take[None, :], axis=1)
    first = jnp.sum((put[None, :] == put[:, None]) & (ids[None, :] < ids[:, None]), axis=1) == 0
    keep = jnp.sum(hot * jnp.where(first, 0, 1)[None, :], axis=1)
    outs = jnp.arange(16, dtype=jnp.int32)
    here = jnp.sum((put[None, :] == outs[:, None]).astype(jnp.int32), axis=1)
    upto = jnp.sum((put[None, :] <= outs[:, None]).astype(jnp.int32), axis=1)
    last = jnp.where(here > 0, upto - 1, n)
    return jnp.concatenate([order, takes, keep, last])


class Ring:
    def __init__(self, ring, pair, slot, device):
        self.ring, self.pair = ring, pair
        self.slot_of, self.device_of = slot, device

    def at(self, dr, dp):
        return lax.rem(self.ring + dr, 4), (1 - self.pair) if dp else self.pair

    def slot(self, dr, dp, **kw):
        return self.slot_of(*self.at(dr, dp), **kw)

    def device(self, dr, dp):
        return self.device_of(*self.at(dr, dp))


class Net:
    def __init__(self, send_sems, recv_sems):
        self.send_sems, self.recv_sems = send_sems, recv_sems
        self.names, self.sends = {}, {}
        self.open = {}

    def send(self, src, dst, device, group, name):
        i = self.names.setdefault(name, len(self.names))
        now = self.open.setdefault(group, [])
        j = self.sends.setdefault((group, len(now)), len(self.sends))
        copy = pltpu.make_async_remote_copy(
            src_ref=src,
            dst_ref=dst,
            send_sem=self.send_sems.at[j],
            recv_sem=self.recv_sems.at[i],
            device_id=device,
            device_id_type=MESH,
        )
        copy.start()
        now.append(copy)
        return copy

    def arrived(self, ref, device, name):
        pltpu.make_async_remote_copy(
            src_ref=ref,
            dst_ref=ref,
            send_sem=self.send_sems.at[0],
            recv_sem=self.recv_sems.at[self.names[name]],
            device_id=device,
            device_id_type=MESH,
        ).wait_recv()

    def drain(self, group):
        for copy in self.open.pop(group, []):
            copy.wait_send()


def gather(net, geo, x, key, group, direct, partner=None):
    half = x.shape[1] // 2
    low, high = pl.ds(0, half), pl.ds(half, half)
    right, left, pair, far = geo.device(1, 0), geo.device(3, 0), geo.device(0, 1), geo.device(2, 0)
    net.drain(group)

    def send(ref, device, name):
        return net.send(ref, ref, device, group, (key, name))

    def share(dr, dp):
        if partner is not None:
            send(x.at[geo.slot(dr, dp)], partner, "share")

    mine, his = x.at[geo.slot(0, 0)], x.at[geo.slot(0, 1)]
    across = send(mine, pair, "across")
    own_r, own_l = send(mine, right, "own_r"), send(mine, left, "own_l")
    share(0, 0)
    yield
    own_r.wait_recv()
    far_a = send(x.at[geo.slot(3, 0), low], right, "far_a")
    own_l.wait_recv()
    far_b = send(x.at[geo.slot(1, 0), high], left, "far_b")
    share(3, 0)
    share(1, 0)
    yield
    across.wait_recv()
    other = [send(his, right, "other_r"), send(his, left, "other_l")]
    if direct:
        other.append(send(his, far, "other_f"))
    share(0, 1)
    yield
    far_a.wait_recv()
    far_b.wait_recv()
    if not direct:
        other.append(send(x.at[geo.slot(2, 0)], pair, "other_f"))
    share(2, 0)
    yield
    for c, dr in zip(other, (3, 1, 2)):
        c.wait_recv()
        share(dr, 1)
    yield
    if partner is not None:
        net.arrived(x.at[pl.ds(0, 8)], partner, (key, "share"))
    yield


ORDER = ((2, 1), (1, 1), (3, 1), (1, 0), (3, 0), (2, 0), (0, 1), (0, 0))
GROUPS = ((0, 1), (1, 4), (5, 1), (6, 2))


def place(dr, dp):
    return ORDER.index((dr, dp))


def scatter(net, geo, pick, s, buf, key, group, done, direct, partner=None, t=None, rc=None):
    ra, rp, rq, rd, total = buf
    half = s.shape[1] // 2
    low, high = pl.ds(0, half), pl.ds(half, half)
    right, left, pair, far = geo.device(1, 0), geo.device(3, 0), geo.device(0, 1), geo.device(2, 0)
    net.drain(group)

    def send(src, dst, device, name):
        return net.send(src, dst, device, group, (key, name))

    cores = []
    if partner is not None:
        for g, (begin, count) in enumerate(GROUPS):
            for i in range(begin, begin + count):
                t[i] = pick(geo.slot(*ORDER[i], other=True))
            there = pl.ds(begin, count)
            cores.append(send(t.at[there], rc.at[there], partner, ("core", g)))

    def bring(g):
        for i in range(GROUPS[g][0], sum(GROUPS[g])):
            s[i] = pick(geo.slot(*ORDER[i]))

    def add(g):
        if partner is not None:
            cores[g].wait_recv()
            for i in range(GROUPS[g][0], sum(GROUPS[g])):
                s[i] = (s[i].astype(F32) + rc[i].astype(F32)).astype(BF)

    def send_other():
        if direct:
            send(s.at[place(2, 1)], rq.at[2], far, "q")
        else:
            send(s.at[place(2, 1)], rq.at[2], pair, "far")

    def send_near():
        send(s.at[place(1, 1)], rq.at[0], right, "q")
        send(s.at[place(3, 1)], rq.at[1], left, "q")
        send(s.at[place(1, 0), high], rp.at[0, 1], right, "p")
        send(s.at[place(3, 0), low], rp.at[1, 0], left, "p")

    def send_far():
        i = place(2, 0)
        if not direct:
            net.arrived(rq.at[2], pair, (key, "far"))
            s[i] = (s[i].astype(F32) + rq[2].astype(F32)).astype(BF)
        return send(s.at[i, low], ra.at[0], right, "a"), send(s.at[i, high], ra.at[1], left, "b")

    if partner is None:
        bring(0)
        send_other()
        bring(1)
        send_near()
        bring(2)
        bring(3)
        yield
        yield
        first = send_far()
    else:
        for g in range(4):
            bring(g)
        yield
        add(0)
        send_other()
        add(1)
        send_near()
        yield
        add(2)
        first = send_far()
        add(3)
    yield
    i = place(0, 1)
    if direct:
        net.arrived(rq, pair, (key, "q"))
        s[i] = (s[i].astype(F32) + rq[0].astype(F32) + rq[1].astype(F32) + rq[2].astype(F32)).astype(BF)
    else:
        net.arrived(rq.at[pl.ds(0, 2)], pair, (key, "q"))
        s[i] = (s[i].astype(F32) + rq[0].astype(F32) + rq[1].astype(F32)).astype(BF)
    last = send(s.at[i], rd, pair, "last")
    yield
    to_r, to_l = place(1, 0), place(3, 0)
    first[0].wait_recv()
    s[to_r, low] = (s[to_r, low].astype(F32) + ra[0].astype(F32)).astype(BF)
    send(s.at[to_r, low], rp.at[0, 0], right, "p")
    first[1].wait_recv()
    s[to_l, high] = (s[to_l, high].astype(F32) + ra[1].astype(F32)).astype(BF)
    send(s.at[to_l, high], rp.at[1, 1], left, "p")
    yield
    net.arrived(rp, pair, (key, "p"))
    for h, rows in enumerate((low, high)):
        total[rows] = s[place(0, 0), rows].astype(F32) + rp[0, h].astype(F32) + rp[1, h].astype(F32)
    yield
    last.wait_recv()
    done(total[...] + rd[...].astype(F32))
    yield


def all_reduce(net, g, bufs, where, out, key):
    x, y, z, core, dev_x, dev_yz, partner = where
    b1, r1, h1, b2, r2, h2, b3, r3, gb = bufs
    n, m, w = h1.shape[0], h2.shape[0], b3.shape[2]
    plane = [(dy, dz) for dy in range(4) for dz in range(4) if (dy, dz) != (0, 0)]
    here = y * 4 + z

    def there(dy, dz):
        return lax.rem(y + dy, 4) * 4 + lax.rem(z + dz, 4)

    mine = pl.ds(pl.multiple_of(core * n, n), n)
    his = pl.ds(pl.multiple_of((1 - core) * n, n), n)
    b1[...] = g[his, :].astype(BF)
    c = net.send(b1, r1, partner, "g", (key, 1))
    yield
    c.wait_recv()
    h1[...] = g[mine, :] + r1[...].astype(F32)
    for k in range(16):
        b2[k] = h1[k * m : (k + 1) * m, :].astype(BF)
    for k, d in enumerate(plane):
        net.send(b2.at[there(*d)], r2.at[k], dev_yz(*d), "g", (key, 2))
    yield
    net.arrived(r2, partner, (key, 2))
    total = h1[pl.ds(pl.multiple_of(here * m, m), m), :]
    for k in range(15):
        total = total + r2[k].astype(F32)
    h2[...] = total
    for k in range(4):
        b3[k] = h2[:, k * w : (k + 1) * w].astype(BF)
    for d in (1, 2, 3):
        net.send(b3.at[lax.rem(x + d, 4)], r3.at[d - 1], dev_x(d), "g", (key, 3))
    yield
    net.arrived(r3, partner, (key, 3))
    piece = h2[:, pl.ds(pl.multiple_of(x * w, w), w)]
    piece = piece + r3[0].astype(F32) + r3[1].astype(F32) + r3[2].astype(F32)
    gb[core, here, x] = piece.astype(BF)
    ref = gb.at[core, here, x]
    for d in (1, 2, 3):
        net.send(ref, ref, dev_x(d), "g", (key, 4))
    yield
    net.arrived(gb.at[0, 0, pl.ds(0, 3)], partner, (key, 4))
    ref_p = gb.at[core, here]
    for d in plane:
        net.send(ref_p, ref_p, dev_yz(*d), "g", (key, 5))
    yield
    net.arrived(gb.at[0, pl.ds(0, 15)], partner, (key, 5))
    ref_c = gb.at[core]
    c = net.send(ref_c, ref_c, partner, "g", (key, 6))
    yield
    c.wait_recv()

    def write(i, carry):
        for k in range(4):
            begin = pl.multiple_of(i * m, m)
            out[pl.ds(begin, m), k * w : (k + 1) * w] = gb[i // 16, lax.rem(i, 16), k]
        return carry

    lax.fori_loop(0, 32, write, 0, unroll=4)
    yield


def slope(pre):
    sig = jax.nn.sigmoid(pre)
    return sig * (1.0 + pre * (1.0 - sig))


def dot_rows(a, b):
    return lax.dot_general(a, b, (((0,), (0,)), ((), ())), preferred_element_type=F32)


def dot_cols(a, b):
    return lax.dot_general(a, b, (((1,), (1,)), ((), ())), preferred_element_type=F32)


def dot(a, b):
    return jnp.dot(a, b, preferred_element_type=F32)


WIDTHS = (256, 256)
PROGRAM = (
    "O0", "O1", "F", "H0", "Q0", "S", "H1", "K0", "Q1", "E0", "K1", "G0", "S", "T0", "P0", "U0", "E1", "G1",
    "T1", "P1", "S", "V0", "U1", "V1", "C0", "B0", "S", "D0", "C1", "B1", "Z0", "S", "D1", "S", "Z1",
)
GATHER_DIRECT = (False, False)
SCATTER_DIRECT = (False, False)
SETS = {"f1": 0, "f2": 1, "b2": 0, "b1": 1}
UNROLL = 8


def kernel(names, plan, features, values_hbm, w_first_hbm, w_second_hbm, cotangent_hbm,
           out_act, grad_input, grad_first, grad_second, *scratch):
    m = dict(zip(names, scratch))
    row, col = lax.axis_index("row"), lax.axis_index("col")
    y, zl = row // 2, lax.rem(row, 2)
    zh, x, core = col // 8, lax.rem(col // 2, 4), lax.rem(col, 2)
    z = zh * 2 + zl

    def col_slot(r, p, other=False):
        return p * 8 + r * 2 + ((1 - core) if other else core)

    rows = Ring(y, zl, lambda r, p: r * 2 + p, lambda r, p: (r * 2 + p, col))
    cols = Ring(x, zh, col_slot, lambda r, p: (row, col_slot(r, p)))
    partner = (row, col_slot(x, zh, other=True))

    def dev_x(d):
        return cols.device(d, 0)

    def dev_yz(dy, dz):
        there = lax.rem(z + dz, 4)
        return (lax.rem(y + dy, 4) * 2 + lax.rem(there, 2), col_slot(x, there // 2))

    w_first, w_second, cotangent = m["w1"], m["w2"], m["cot"]
    loads = [
        pltpu.make_async_copy(src, dst, m["load_sems"].at[i])
        for i, (src, dst) in enumerate(
            ((values_hbm, m["a"]), (w_first_hbm, w_first), (w_second_hbm, w_second), (cotangent_hbm, cotangent))
        )
    ]

    barrier = pltpu.get_barrier_semaphore()
    peers = [dev_x(d) for d in (1, 2, 3)] + [partner]
    peers += [dev_yz(dy, dz) for dy in range(4) for dz in range(4) if (dy, dz) != (0, 0)]
    for peer in peers:
        pl.semaphore_signal(barrier, inc=1, device_id=peer, device_id_type=MESH)
    for load in loads:
        load.start()

    net = Net(m["send_sems"], m["recv_sems"])
    nl, width = features.shape
    chunks, begin = [], 0
    for w in WIDTHS:
        chunks.append(slice(begin, begin + w))
        begin += w
    n_chunks = len(chunks)
    n_slots = m["a"].shape[0]
    for w in sorted(set(WIDTHS)):
        prod = m["prod", w]
        prod[n_slots] = jnp.zeros(prod.shape[1:], BF)

    def tile(a, xc, base, w):
        prod, acc = m["prod", w], m["acc", w]
        acc[...] = jnp.zeros_like(acc)

        def step(i, carry):
            p = dot(a[plan[base + i]], xc[plan[base + n_slots + i]])
            v = jnp.where(plan[base + 2 * n_slots + i] > 0, acc[...], 0.0) + p
            acc[...] = v
            prod[i] = v.astype(BF)
            return carry

        lax.fori_loop(0, n_slots, step, 0, unroll=UNROLL)

    reduces = []

    def side(steps=1):
        for _ in range(steps):
            for g in reduces:
                next(g, None)

    def aggregate(name, back, own, filler, done):
        a = m["at"] if back else m["a"]
        base = 3 * n_slots + 16 if back else 0
        geo_in, geo_out = (cols, rows) if back else (rows, cols)
        k = SETS[name]
        ag, rs = [], []
        for c, w in enumerate(WIDTHS):
            def pick(slot, prod=m["prod", w]):
                return prod[plan[base + 3 * n_slots + slot]]

            ag.append(
                gather(net, geo_in, m["x", name, c], ("x", k, c), ("x", c), GATHER_DIRECT[c], partner if back else None)
            )
            more = {} if back else {"partner": partner, "t": m["t", c], "rc": m["rc", name, c]}
            bufs = tuple(m[q, name, c] for q in ("ra", "rp", "rq", "rd")) + (m["total", c],)
            rs.append(
                scatter(
                    net, geo_out, pick, m["s", c], bufs, ("s", k, c), ("s", c),
                    functools.partial(done, c), SCATTER_DIRECT[c], **more,
                )
            )
        for word in PROGRAM:
            c = int(word[1:] or 0)
            if word[0] == "O":
                m["x", name, c][geo_in.slot(0, 0)] = own(c).astype(BF)
                if name == "f1" and c == 0:
                    pl.semaphore_wait(barrier, len(peers))
                next(ag[c])
            elif word[0] in "HQKEG":
                next(ag[c])
            elif word[0] == "T":
                tile(a, m["x", name, c], base, WIDTHS[c])
            elif word[0] == "S":
                side()
            elif word[0] == "F":
                filler()
            else:
                next(rs[c])

    agg, pre_first, pre_second, d_second, d_first = (m[q] for q in ("agg", "pre1", "pre2", "d2", "d1"))

    def layer(k, pre, w):
        def done(c, value):
            agg[k, :, chunks[c]] = value.astype(BF)
            part = dot(agg[k, :, chunks[c]], w[chunks[c], :])
            pre[...] = part if c == 0 else pre[...] + part

        return done

    def wait_loads():
        for load in loads:
            load.wait()

    aggregate("f1", False, lambda c: features[:, chunks[c]], wait_loads, layer(0, pre_first, w_first))

    def turn():
        def one(i, carry):
            m["at"][i] = m["a"][i].T
            return carry

        lax.fori_loop(0, n_slots, one, 0)

    aggregate(
        "f2", False, lambda c: jax.nn.silu(pre_first[:, chunks[c]]), turn, layer(1, pre_second, w_second)
    )
    for c in chunks:
        u = pre_second[:, c]
        d_second[:, c] = (cotangent[:, c].astype(F32) * slope(u)).astype(BF)

    where = (x, y, z, core, dev_x, dev_yz, partner)

    def weight_grad(k, d, out, name):
        g = m["grad", name]
        half = width // 2
        for c in (slice(0, half), slice(half, width)):
            g[c, :] = dot_rows(agg[k, :, c], d[...])
        reduces.append(all_reduce(net, g, [m[q, name] for q in AR_KEYS], where, out, ("g", name)))
        side()

    def hidden_back(c, value):
        d_first[:, chunks[c]] = (value * slope(pre_first[:, chunks[c]])).astype(BF)

    def second_grad():
        out_act[...] = jax.nn.silu(pre_second[...]).astype(BF)
        weight_grad(1, d_second, grad_second, "g2")

    aggregate("b2", True, lambda c: dot_cols(d_second[...], w_second[chunks[c], :]), second_grad, hidden_back)

    def input_back(c, value):
        grad_input[:, chunks[c]] = value.astype(BF)

    aggregate(
        "b1", True, lambda c: dot_cols(d_first[...], w_first[chunks[c], :]),
        lambda: weight_grad(0, d_first, grad_first, "g1"), input_back,
    )
    side(12)
    for group in list(net.open):
        net.drain(group)


AR_KEYS = ("b1", "r1", "h1", "b2", "r2", "h2", "b3", "r3", "gb")


def scratch_of(nl, width, side, slots):
    s = {}

    def add(key, shape, kind=BF):
        s[key] = pltpu.VMEM(shape, kind)

    add("a", (slots, side, side))
    add("at", (slots, side, side))
    add("w1", (width, width))
    add("w2", (width, width))
    add("cot", (nl, width))
    for w in sorted(set(WIDTHS)):
        add(("prod", w), (slots + 1, side, w))
        add(("acc", w), (side, w), F32)
    for c, w in enumerate(WIDTHS):
        add(("s", c), (8, nl, w))
        add(("t", c), (8, nl, w))
        add(("total", c), (nl, w), F32)
        for name, blocks in (("f1", 8), ("f2", 8), ("b2", 16), ("b1", 16)):
            add(("x", name, c), (blocks, nl, w))
            add(("ra", name, c), (2, nl // 2, w))
            add(("rp", name, c), (2, 2, nl // 2, w))
            add(("rq", name, c), (3, nl, w))
            add(("rd", name, c), (nl, w))
            if blocks == 8:
                add(("rc", name, c), (8, nl, w))
    add("agg", (2, nl, width))
    add("pre1", (nl, width), F32)
    add("pre2", (nl, width), F32)
    add("d2", (nl, width))
    add("d1", (nl, width))
    h = width
    for name in ("g2", "g1"):
        add(("grad", name), (width, width), F32)
        add(("b1", name), (h // 2, width))
        add(("r1", name), (h // 2, width))
        add(("h1", name), (h // 2, width), F32)
        add(("b2", name), (16, h // 32, width))
        add(("r2", name), (15, h // 32, width))
        add(("h2", name), (h // 32, width), F32)
        add(("b3", name), (4, h // 32, width // 4))
        add(("r3", name), (3, h // 32, width // 4))
        add(("gb", name), (2, 16, 4, h // 32, width // 4))
    s["load_sems"] = pltpu.SemaphoreType.DMA((4,))
    n = len(WIDTHS)
    s["send_sems"] = pltpu.SemaphoreType.DMA((30 * n + 76,))
    s["recv_sems"] = pltpu.SemaphoreType.DMA((38 * n + 14,))
    return s


def tail(out_act, grad_input, grad_first, grad_second, out_act_t, grad_input_t, grad_first_t, grad_second_t):
    out_act_t[...] = out_act[...]
    grad_input_t[...] = grad_input[...]
    grad_first_t[...] = grad_first[...].astype(F32)
    grad_second_t[...] = grad_second[...].astype(F32)


def local(features, adj_values, block_cells, block_counts, w_first, w_second, cotangent):
    values, cells, live = adj_values[0, 0], block_cells[0, 0], block_counts[0, 0]
    nl, width = features.shape
    slots, side, _ = values.shape
    plan = jnp.concatenate([slot_plan(cells, live, 8, 16, False), slot_plan(cells, live, 8, 8, True)])
    scratch = scratch_of(nl, width, side, slots)
    vmem = pl.BlockSpec(memory_space=pltpu.VMEM)
    hbm = pl.BlockSpec(memory_space=pl.ANY)

    def shapes(kind):
        node, weight = jax.ShapeDtypeStruct((nl, width), BF), jax.ShapeDtypeStruct((width, width), kind)
        return (node, node, weight, weight)

    outs = pl.pallas_call(
        functools.partial(kernel, tuple(scratch)),
        out_shape=shapes(BF),
        in_specs=[pl.BlockSpec(memory_space=pltpu.SMEM), vmem, hbm, hbm, hbm, hbm],
        out_specs=(vmem, vmem, vmem, vmem),
        scratch_shapes=list(scratch.values()),
        compiler_params=pltpu.CompilerParams(
            collective_id=0, has_side_effects=True, vmem_limit_bytes=63 * 1024 * 1024 - 512 * 1024
        ),
    )(plan, features, values, w_first, w_second, cotangent)
    return pl.pallas_call(
        tail,
        out_shape=shapes(F32),
        in_specs=[vmem] * 4,
        out_specs=(vmem,) * 4,
        compiler_params=pltpu.CompilerParams(vmem_limit_bytes=16 * 1024 * 1024),
    )(*outs)


def solution(mesh):
    return jax.shard_map(
        local,
        mesh=mesh,
        in_specs=(
            P(("row", "col"), None),
            P("row", "col", None, None, None),
            P("row", "col", None),
            P("row", "col"),
            P(),
            P(),
            P(("row", "col"), None),
        ),
        out_specs=(P(("row", "col"), None), P(("row", "col"), None), P(), P()),
        check_vma=False,
    )
```

time: 1600 us -> 183 us (0.11)
  waiting for transfers between devices: 1040 us -> 0 us
  loops' own time: 338 us -> 0 us
  Pallas kernels: 0 us -> 175 us
  local copies, waits for them, and re-layouts: 90.6 us -> 4.63 us
  matrix products: 81.7 us -> 0 us
  other arithmetic: 21.7 us -> 1.74 us
    reduce_scatter x4 -> x0, waiting for transfers between devices: 795 us -> none  [the longest x2 442 us: aggregate(): lax.psum_scatter(partial_value.astype(jnp.bfloat16), 'col', scatter_dimen...]
    another operation x132 -> x0, loops' own time: 338 us -> none  [the longest x4 245 us: tile_range(): return lax.fori_loop(0, finish, advance, start)]
    all_gather x4 -> x0, waiting for transfers between devices: 215 us -> none  [the longest x2 112 us: aggregate_back(): lax.all_gather(local_rows, 'col', axis=0, tiled=True)]
    pallas_call x0 -> x2, Pallas kernels: none -> 175 us  [the longest x1 173 us: local(): pl.pallas_call(functools.partial(kernel, tuple(scratch)), out_shape=shape...]
    dot_general x42 -> x0, matrix products: 81.7 us -> none  [the longest x18 37.7 us: add_block(): lax.dot_general(block, picked, (((0,), (0,)), ((), ())), preferred_elemen...]
    dynamic_slice x88 -> x0, local copies, waits for them, and re-layouts: 72.1 us -> none  [the longest x36 38.9 us: add_block(): old = lax.dynamic_index_in_dim(current, place, 0, keepdims=False)]
    psum x1 -> x0, waiting for transfers between devices: 26.1 us -> none  [local(): grad_first = lax.psum(local_first, ('row', 'col'))]
    convert_element_type x5 -> x0, other arithmetic: 21 us -> none  [the longest x2 12.1 us: aggregate(): partial_value.astype(jnp.bfloat16)]
  transfers between devices with their start and end apart: 9 -> 0, of which waited for: 9 -> 0; matrix products, arithmetic and copies ran while one was open for 3% -> 0% of each run, Pallas kernels for 0% -> 0%
where the time goes in v2:
time: 183 us
  Pallas kernels  175 us (96%)
  local copies, waits for them, and re-layouts  4.63 us (3%)
    pallas_call x1, Pallas kernels, local(): pl.pallas_call(functools.partial(kernel, tuple(scratch)), out_shape=shape...  173 us
    unnamed x8, local copies, waits for them, and re-layouts  3.97 us

profile of v2, /device:TPU:1, one launch (start us, length us, event | category | flops | bytes accessed | tf_op | source)
XLA Modules:
  0.0 182.5 jit_solution(1076721594372274041)
XLA Ops:
  1.3 0.7 iota_add_fusion
  1.9 0.2 convert_reduce_fusion.1
  2.1 0.2 convert_reduce_fusion.3
  2.3 0.2 convert_reduce_fusion
  2.5 0.2 convert_reduce_fusion.2
  2.7 0.2 select_reduce_fusion
  2.9 0.2 convert_reduce_fusion.4
  3.1 0.7 concatenate.3.plan
  3.7 173.3 %shard_map.102 = (bf16[256,512]{1,0:T(8,128)(2,1)}, bf16[256,512]{1,0:T(8,128)(2,1)}, bf16[512,512]{1,0:T(8,128)(2,1)}, bf16[512,512]{1,0:T(8,128)(2,1)}) custom-call(s32[224]{0:T(256)} %concatenate.3.plan, bf16[256,512]{1,0:T(8,128)(2,1)} %features.1, bf16[32,256,256]{2,1,0:T(8,128)(2,1)} %bitcast.20, bf16[512,512]{1,0:T(8,128)(2,1)} %w_first_hbm.1, ...), custom_call_target="tpu_custom_call" | custom-call | tf_op jit(solution)/shard_map/pallas_call | solution.py:569
  177.0 0.0 copy-start
  177.0 1.0 copy-done
  178.1 0.0 copy-start.1
  178.1 1.0 copy-done.1
  179.1 0.0 copy-start.2
  179.1 0.9 copy-done.2
  180.0 0.0 copy-start.3
  180.0 0.9 copy-done.3
  181.0 1.5 shard_map.103
  (4 shorter events, 0.0 us)
Async XLA Ops:
  177.0 1.0 copy-start
  178.1 1.0 copy-start.1
  179.1 0.9 copy-start.2
  180.0 0.9 copy-start.3

commit v3 on v2

--- a/solution.py
+++ b/solution.py
@@ -12,24 +12,34 @@
 F32 = jnp.float32
 
 
-def slot_plan(cells, live_count, block_cols, n_out, transposed):
-    n = cells.shape[0]
-    ids = jnp.arange(n, dtype=jnp.int32)
-    rows, cols = cells // block_cols, cells % block_cols
-    take, put = (rows, cols) if transposed else (cols, rows)
-    put = jnp.where(ids < live_count, put, n_out)
-    key = put * n + ids
-    rank = jnp.sum((key[None, :] < key[:, None]).astype(jnp.int32), axis=1)
-    hot = (rank[None, :] == ids[:, None]).astype(jnp.int32)
-    order = jnp.sum(hot * ids[None, :], axis=1)
-    takes = jnp.sum(hot * take[None, :], axis=1)
-    first = jnp.sum((put[None, :] == put[:, None]) & (ids[None, :] < ids[:, None]), axis=1) == 0
-    keep = jnp.sum(hot * jnp.where(first, 0, 1)[None, :], axis=1)
-    outs = jnp.arange(16, dtype=jnp.int32)
-    here = jnp.sum((put[None, :] == outs[:, None]).astype(jnp.int32), axis=1)
-    upto = jnp.sum((put[None, :] <= outs[:, None]).astype(jnp.int32), axis=1)
-    last = jnp.where(here > 0, upto - 1, n)
-    return jnp.concatenate([order, takes, keep, last])
+def slot_plan(cells, live, out, base, n_out, transposed):
+    n = cells.shape[1]
+    lane = lax.broadcasted_iota(jnp.int32, (n, n), 1)
+    line = lax.broadcasted_iota(jnp.int32, (n, n), 0)
+    cell = jnp.broadcast_to(cells[...], (n, n))
+
+    def column(a):
+        return jnp.sum(jnp.where(lane == line, a, 0), axis=1, keepdims=True)
+
+    def line_sum(where, a):
+        return jnp.sum(jnp.where(where, a, 0), axis=0, keepdims=True)
+
+    def count(where):
+        return jnp.sum(jnp.where(where, 1, 0), axis=1, keepdims=True)
+
+    take, put = lax.bitwise_and(cell, 7), lax.shift_right_logical(cell, 3)
+    if transposed:
+        take, put = put, take
+    put = jnp.where(lane < live, put, n_out)
+    key = put * n + lane
+    rank = count(key < column(key))
+    hot = rank == lane
+    again = count((put == column(put)) & (lane < line))
+    last = jnp.where(count(put == line) > 0, count(put <= line) - 1, n)
+    out[base : base + 1, 0:n] = line_sum(hot, line)
+    out[base + 1 : base + 2, 0:n] = line_sum(hot, column(take))
+    out[base + 2 : base + 3, 0:n] = line_sum(hot, again)
+    out[base + 3 : base + 4, 0:n] = line_sum(lane == line, last)
 
 
 class Ring:
@@ -312,18 +322,19 @@
     return jnp.dot(a, b, preferred_element_type=F32)
 
 
-WIDTHS = (256, 256)
+WIDTHS = (128, 256, 128)
 PROGRAM = (
-    "O0", "O1", "F", "H0", "Q0", "S", "H1", "K0", "Q1", "E0", "K1", "G0", "S", "T0", "P0", "U0", "E1", "G1",
-    "T1", "P1", "S", "V0", "U1", "V1", "C0", "B0", "S", "D0", "C1", "B1", "Z0", "S", "D1", "S", "Z1",
+    "O0", "O1", "F", "H0", "Q0", "O2", "S", "H1", "Q1", "K0", "H2", "K1", "Q2", "E0", "G0", "S", "T0", "P0",
+    "K2", "U0", "E1", "G1", "S", "T1", "P1", "V0", "U1", "E2", "G2", "T2", "P2", "V1", "U2", "C0", "S", "B0",
+    "V2", "C1", "B1", "S", "D0", "C2", "B2", "Z0", "D1", "Z1", "S", "D2", "Z2",
 )
-GATHER_DIRECT = (False, False)
-SCATTER_DIRECT = (False, False)
+GATHER_DIRECT = (False, False, False)
+SCATTER_DIRECT = (False, False, False)
 SETS = {"f1": 0, "f2": 1, "b2": 0, "b1": 1}
 UNROLL = 8
 
 
-def kernel(names, plan, features, values_hbm, w_first_hbm, w_second_hbm, cotangent_hbm,
+def kernel(names, cells, live, features, values_hbm, w_first_hbm, w_second_hbm, cotangent_hbm,
            out_act, grad_input, grad_first, grad_second, *scratch):
     m = dict(zip(names, scratch))
     row, col = lax.axis_index("row"), lax.axis_index("col")
@@ -345,7 +356,7 @@
         there = lax.rem(z + dz, 4)
         return (lax.rem(y + dy, 4) * 2 + lax.rem(there, 2), col_slot(x, there // 2))
 
-    w_first, w_second, cotangent = m["w1"], m["w2"], m["cot"]
+    w_first, w_second, cotangent, plan = m["w1"], m["w2"], m["cot"], m["plan"]
     loads = [
         pltpu.make_async_copy(src, dst, m["load_sems"].at[i])
         for i, (src, dst) in enumerate(
@@ -378,8 +389,8 @@
         acc[...] = jnp.zeros_like(acc)
 
         def step(i, carry):
-            p = dot(a[plan[base + i]], xc[plan[base + n_slots + i]])
-            v = jnp.where(plan[base + 2 * n_slots + i] > 0, acc[...], 0.0) + p
+            p = dot(a[plan[base, i]], xc[plan[base + 1, i]])
+            v = jnp.where(plan[base + 2, i] > 0, acc[...], 0.0) + p
             acc[...] = v
             prod[i] = v.astype(BF)
             return carry
@@ -395,13 +406,13 @@
 
     def aggregate(name, back, own, filler, done):
         a = m["at"] if back else m["a"]
-        base = 3 * n_slots + 16 if back else 0
+        base = 4 if back else 0
         geo_in, geo_out = (cols, rows) if back else (rows, cols)
         k = SETS[name]
         ag, rs = [], []
         for c, w in enumerate(WIDTHS):
             def pick(slot, prod=m["prod", w]):
-                return prod[plan[base + 3 * n_slots + slot]]
+                return prod[plan[base + 3, slot]]
 
             ag.append(
                 gather(net, geo_in, m["x", name, c], ("x", k, c), ("x", c), GATHER_DIRECT[c], partner if back else None)
@@ -443,6 +454,11 @@
         return done
 
     def wait_loads():
+        slot_plan(cells, live[0, 0], m["lines"], 0, 16, False)
+        slot_plan(cells, live[0, 0], m["lines"], 4, 8, True)
+        move = pltpu.make_async_copy(m["lines"], plan, m["load_sems"].at[4])
+        move.start()
+        move.wait()
         for load in loads:
             load.wait()
 
@@ -539,7 +555,9 @@
         add(("b3", name), (4, h // 32, width // 4))
         add(("r3", name), (3, h // 32, width // 4))
         add(("gb", name), (2, 16, 4, h // 32, width // 4))
-    s["load_sems"] = pltpu.SemaphoreType.DMA((4,))
+    s["lines"] = pltpu.VMEM((8, 128), jnp.int32)
+    s["plan"] = pltpu.SMEM((8, 128), jnp.int32)
+    s["load_sems"] = pltpu.SemaphoreType.DMA((5,))
     n = len(WIDTHS)
     s["send_sems"] = pltpu.SemaphoreType.DMA((30 * n + 76,))
     s["recv_sems"] = pltpu.SemaphoreType.DMA((38 * n + 14,))
@@ -554,10 +572,9 @@
 
 
 def local(features, adj_values, block_cells, block_counts, w_first, w_second, cotangent):
-    values, cells, live = adj_values[0, 0], block_cells[0, 0], block_counts[0, 0]
+    values, cells = adj_values[0, 0], block_cells[0]
     nl, width = features.shape
     slots, side, _ = values.shape
-    plan = jnp.concatenate([slot_plan(cells, live, 8, 16, False), slot_plan(cells, live, 8, 8, True)])
     scratch = scratch_of(nl, width, side, slots)
     vmem = pl.BlockSpec(memory_space=pltpu.VMEM)
     hbm = pl.BlockSpec(memory_space=pl.ANY)
@@ -569,13 +586,13 @@
     outs = pl.pallas_call(
         functools.partial(kernel, tuple(scratch)),
         out_shape=shapes(BF),
-        in_specs=[pl.BlockSpec(memory_space=pltpu.SMEM), vmem, hbm, hbm, hbm, hbm],
+        in_specs=[vmem, pl.BlockSpec(memory_space=pltpu.SMEM), vmem, hbm, hbm, hbm, hbm],
         out_specs=(vmem, vmem, vmem, vmem),
         scratch_shapes=list(scratch.values()),
         compiler_params=pltpu.CompilerParams(
             collective_id=0, has_side_effects=True, vmem_limit_bytes=63 * 1024 * 1024 - 512 * 1024
         ),
-    )(plan, features, values, w_first, w_second, cotangent)
+    )(cells, block_counts, features, values, w_first, w_second, cotangent)
     return pl.pallas_call(
         tail,
         out_shape=shapes(F32),

time: 183 us -> 172 us (0.940)
  Pallas kernels: 175 us -> 167 us
    pallas_call x1, Pallas kernels: 173 us -> 165 us  [local(): pl.pallas_call(functools.partial(kernel, tuple(scratch)), out_shape=shape...]
where the time goes in v3:
time: 172 us
  Pallas kernels  167 us (97%)
  local copies, waits for them, and re-layouts  3.97 us (2%)
    pallas_call x1, Pallas kernels, local(): pl.pallas_call(functools.partial(kernel, tuple(scratch)), out_shape=shape...  165 us
    unnamed x8, local copies, waits for them, and re-layouts  3.97 us

profile of v3, /device:TPU:1, one launch (start us, length us, event | category | flops | bytes accessed | tf_op | source)
XLA Modules:
  0.0 172.0 jit_solution(2847603422484339965)
XLA Ops:
  1.3 165.2 %shard_map.102 = (bf16[256,512]{1,0:T(8,128)(2,1)}, bf16[256,512]{1,0:T(8,128)(2,1)}, bf16[512,512]{1,0:T(8,128)(2,1)}, bf16[512,512]{1,0:T(8,128)(2,1)}) custom-call(s32[1,32]{1,0:T(1,128)} %bitcast.3, s32[1,1]{1,0:T(1,128)S(6)} %copy.11.live, bf16[256,512]{1,0:T(8,128)(2,1)} %features.1, bf16[32,256,256]{2,1,0:T(8,128)(2,1)} %bitcast.2, ...), custom_call_target="tpu_custom_call" | custom-call | tf_op jit(solution)/shard_map/pallas_call | solution.py:586
  166.5 0.0 copy-start
  166.5 1.0 copy-done
  167.5 0.0 copy-start.1
  167.5 1.0 copy-done.1
  168.5 0.0 copy-start.2
  168.6 0.9 copy-done.2
  169.5 0.0 copy-start.3
  169.5 0.9 copy-done.3
  170.4 1.5 shard_map.103
Async XLA Ops:
  166.5 1.0 copy-start
  167.5 1.0 copy-start.1
  168.5 0.9 copy-start.2
  169.5 0.9 copy-start.3

commit v4 on v3

--- a/solution.py
+++ b/solution.py
@@ -564,11 +564,19 @@
     return s
 
 
-def tail(out_act, grad_input, grad_first, grad_second, out_act_t, grad_input_t, grad_first_t, grad_second_t):
-    out_act_t[...] = out_act[...]
-    grad_input_t[...] = grad_input[...]
-    grad_first_t[...] = grad_first[...].astype(F32)
-    grad_second_t[...] = grad_second[...].astype(F32)
+def tail(
+    out_act, grad_input, grad_first, grad_second, out_act_t, grad_input_t, grad_first_t, grad_second_t, first, second, sems
+):
+    pairs = ((grad_first, first), (grad_second, second), (out_act, out_act_t), (grad_input, grad_input_t))
+    copies = [pltpu.make_async_copy(src, dst, sems.at[i]) for i, (src, dst) in enumerate(pairs)]
+    for copy in copies:
+        copy.start()
+    copies[0].wait()
+    grad_first_t[...] = first[...].astype(F32)
+    copies[1].wait()
+    grad_second_t[...] = second[...].astype(F32)
+    copies[2].wait()
+    copies[3].wait()
 
 
 def local(features, adj_values, block_cells, block_counts, w_first, w_second, cotangent):
@@ -596,9 +604,10 @@
     return pl.pallas_call(
         tail,
         out_shape=shapes(F32),
-        in_specs=[vmem] * 4,
+        in_specs=[hbm] * 4,
         out_specs=(vmem,) * 4,
-        compiler_params=pltpu.CompilerParams(vmem_limit_bytes=16 * 1024 * 1024),
+        scratch_shapes=[pltpu.VMEM((width, width), BF)] * 2 + [pltpu.SemaphoreType.DMA((4,))],
+        compiler_params=pltpu.CompilerParams(vmem_limit_bytes=60 * 1024 * 1024),
     )(*outs)
 
 

time: 172 us -> 170 us (0.988)
  local copies, waits for them, and re-layouts: 3.97 us -> 0 us
    unnamed x8 -> x0, local copies, waits for them, and re-layouts: 3.97 us -> none
where the time goes in v4:
time: 170 us; the launch traced here: 169 us
  Pallas kernels  168 us (99%)
    pallas_call x1, Pallas kernels, local(): pl.pallas_call(functools.partial(kernel, tuple(scratch)), out_shape=shape...  165 us

profile of v4, /device:TPU:1, one launch (start us, length us, event | category | flops | bytes accessed | tf_op | source)
XLA Modules:
  0.0 169.3 jit_solution(5995591626825453021)
XLA Ops:
  1.3 165.2 %shard_map.102 = (bf16[256,512]{1,0:T(8,128)(2,1)}, bf16[256,512]{1,0:T(8,128)(2,1)}, bf16[512,512]{1,0:T(8,128)(2,1)}, bf16[512,512]{1,0:T(8,128)(2,1)}) custom-call(s32[1,32]{1,0:T(1,128)} %bitcast.3, s32[1,1]{1,0:T(1,128)S(6)} %copy.11.live, bf16[256,512]{1,0:T(8,128)(2,1)} %features.1, bf16[32,256,256]{2,1,0:T(8,128)(2,1)} %bitcast.2, ...), custom_call_target="tpu_custom_call" | custom-call | tf_op jit(solution)/shard_map/pallas_call | solution.py:594
  166.5 2.9 %shard_map.103 = (bf16[256,512]{1,0:T(8,128)(2,1)}, bf16[256,512]{1,0:T(8,128)(2,1)}, f32[512,512]{1,0:T(8,128)}, f32[512,512]{1,0:T(8,128)}) custom-call(bf16[256,512]{1,0:T(8,128)(2,1)} %get-tuple-element.8.out_act, bf16[256,512]{1,0:T(8,128)(2,1)} %get-tuple-element.9.grad_input, bf16[512,512]{1,0:T(8,128)(2,1)} %get-tuple-element.10.grad_first, ...), custom_call_target="tpu_custom_call" | custom-call | tf_op jit(solution)/shard_map/pallas_call | solution.py:604
